TPU v7x, 768 devices: a whole 4x8x12 slice. The times are simulated.
768 devices in a mesh: grp: 96 (over y, z), sub: 8 (over x, core).
Axes of the slice: x: 4, y: 8, z: 12, core: 2. Of those that a mesh axis runs over, the one named last changes fastest.
Arguments:
- adjoint: float32 [5, 512, 98304], P(None, None, ('grp', 'sub')), may hold values from -15 to 15
- velocity: float32 [3, 512, 98304], P(None, None, ('grp', 'sub')), may hold values from -6 to 6
- geometry: float32 [4, 98304], P(None, ('grp', 'sub')), may hold values from 0.5 to 2
- face_codes: int32 [768, 704], P(('grp', 'sub')), may hold values from -1 to 767, as said below
Outputs:
- solution: float32 [5, 512, 98304], P(None, None, ('grp', 'sub'))
Inputs may be any that keep to these rules, and one draw needn't show every extreme that they name: `face_codes`: on the device of group g and owner p, slots f and f + 288 of the first block are partners for f < 288, both empty or both live. Then block q holds slots f = 0..15: block p is empty; for q != p, slot f of block q and slot f of block p on the device of group g and owner q are partners and are both empty or both live. No face of an element is named twice in one device's list. In every group some pair of owners has all 16 slots of their blocks live.
All inputs are finite; a program needn't handle non-finite values.
Results may differ from a plain program's by a relative error of at most 0.00045.
Values sent between devices are 32-bit elements; how exact they have to be, the bound alone decides.
A program may use at most 64 MiB of HBM per device.

v0:
```python
import functools

import jax
import jax.numpy as jnp
from jax import lax
from jax.experimental import pallas as pl
from jax.experimental.pallas import tpu as pltpu
from jax.sharding import PartitionSpec as P

MESH = pl.DeviceIdType.MESH
COMP = 5
POINTS = 512
LPAIR = 288
FMAX = 16
FACE_ROWS = 48
HALF_ROWS = 256
TIME_STEP = 0.05
DIFFUSIVITY = (1.0, 1.0, 1.0, 0.7, 0.2)
GLL_POINTS = (
    -1.0,
    -0.8717401485096066,
    -0.5917001814331423,
    -0.2092992179024789,
    0.2092992179024789,
    0.5917001814331423,
    0.8717401485096066,
    1.0,
)


def legendre_seven(point):
    before = 1.0
    current = point
    for order in range(1, 7):
        following = ((2 * order + 1) * point * current - order * before) / (order + 1)
        before = current
        current = following
    return current


def gll_tables():
    points = list(GLL_POINTS)
    values = [legendre_seven(point) for point in points]
    weights = [2.0 / (56.0 * value * value) for value in values]
    derivative = []
    for row in range(8):
        line = []
        for col in range(8):
            if row == col:
                line.append(0.0)
            else:
                line.append(values[row] / (values[col] * (points[row] - points[col])))
        derivative.append(line)
    derivative[0][0] = -14.0
    derivative[7][7] = 14.0
    stiffness = []
    for row in range(8):
        line = []
        for col in range(8):
            total = 0.0
            for mid in range(8):
                total += derivative[mid][row] * weights[mid] * derivative[mid][col]
            line.append(total / weights[row])
        stiffness.append(line)
    return weights, derivative, stiffness


def halves(matrix):
    even = [[0.5 * (matrix[i][a] + matrix[i][7 - a]) for a in range(4)] for i in range(4)]
    odd = [[0.5 * (matrix[i][a] - matrix[i][7 - a]) for a in range(4)] for i in range(4)]
    return even, odd


WEIGHTS, DERIVATIVE, STIFFNESS = gll_tables()
DERIVATIVE_HALVES = halves(DERIVATIVE) + (-1,)
STIFFNESS_HALVES = halves(STIFFNESS) + (1,)


def product(values, table):
    even, odd, sign = table
    sums = [values[a] + values[7 - a] for a in range(4)]
    gaps = [values[a] - values[7 - a] for a in range(4)]
    result = [None] * 8
    for i in range(4):
        first = sum(even[i][a] * sums[a] for a in range(1, 4)) + even[i][0] * sums[0]
        second = sum(odd[i][a] * gaps[a] for a in range(1, 4)) + odd[i][0] * gaps[0]
        result[i] = first + second
        result[7 - i] = first - second if sign > 0 else second - first
    return result


def rows(start):
    return pl.ds(pl.multiple_of(start, 8), 8)


def every_eighth(start):
    return pl.ds(start, 8, stride=8)


def sublane_sum(value):
    return jnp.sum(value, axis=0, keepdims=True)


def split(value):
    high = value.astype(jnp.bfloat16)
    low = (value - high.astype(jnp.float32)).astype(jnp.bfloat16)
    return high, low


def dot(first, second, dims):
    return lax.dot_general(
        first, second, (dims, ((), ())), preferred_element_type=jnp.float32
    )


def face_slice(face, base, step):
    direction, level = face // 2, 7 * (face % 2)
    if direction == 0:
        return pl.ds(pl.multiple_of(base + 64 * level + 8 * step, 8), 8)
    if direction == 1:
        return pl.ds(pl.multiple_of(base + 64 * step + 8 * level, 8), 8)
    return pl.ds(base + 64 * step + level, 8, stride=8)


def kernel(
    sizes,
    adjoint_hbm,
    velocity_hbm,
    geometry_hbm,
    codes_hbm,
    first_hbm,
    image_hbm,
    factor_ref,
    adjoint,
    velocity,
    geometry,
    codes,
    first,
    image,
    mass,
    along_i,
    along_k,
    columns,
    pairs,
    chosen,
    faces,
    gained,
    outgoing,
    incoming,
    partial,
    sub_slots,
    y_slots,
    z_slots,
    load_sem,
    store_sem,
    face_send,
    face_recv,
    sum_send,
    sum_recv,
):
    owners, n_y, n_z = sizes
    me = lax.axis_index("sub")
    group = lax.axis_index("grp")
    my_y = group // n_z
    my_z = group - my_y * n_z

    loads = [pltpu.make_async_copy(codes_hbm, codes, load_sem.at[0])]
    loads.append(pltpu.make_async_copy(geometry_hbm, geometry, load_sem.at[1]))
    loads.append(pltpu.make_async_copy(velocity_hbm, velocity, load_sem.at[2]))
    loads.append(pltpu.make_async_copy(adjoint_hbm, adjoint, load_sem.at[3]))
    for load in loads:
        load.start()

    barrier = pltpu.get_barrier_semaphore()

    def sub_peer(step):
        return lax.rem(me + step, owners)

    def y_peer(step):
        return lax.rem(my_y + step, n_y)

    def z_peer(step):
        return lax.rem(my_z + step, n_z)

    for step in range(1, owners):
        pl.semaphore_signal(barrier, inc=1, device_id={"sub": sub_peer(step)}, device_id_type=MESH)
    for step in range(1, n_y):
        pl.semaphore_signal(
            barrier, inc=1, device_id={"grp": y_peer(step) * n_z + my_z}, device_id_type=MESH
        )
    for step in range(1, n_z):
        pl.semaphore_signal(
            barrier, inc=1, device_id={"grp": my_y * n_z + z_peer(step)}, device_id_type=MESH
        )

    sublane = lax.broadcasted_iota(jnp.int32, (8, 128), 0)
    lane = lax.broadcasted_iota(jnp.int32, (8, 128), 1).astype(jnp.float32)
    inside = jnp.where((sublane >= 1) & (sublane <= 6), 1.0, 0.0)
    depth_weight = jnp.zeros((8, 128), jnp.float32)
    for k in range(8):
        depth_weight = jnp.where(sublane == k, WEIGHTS[k], depth_weight)

    loads[0].wait()
    for tile in range(6):
        width = min(128, 704 - 128 * tile)
        row = codes[:, 128 * tile : 128 * tile + width].astype(jnp.float32)
        columns[128 * tile : 128 * tile + width, :] = jnp.transpose(
            jnp.broadcast_to(row, (128, width))
        )

    def find(index, found):
        here = columns[rows(index * 8), :]
        there = columns[rows(index * 8 + LPAIR), :]
        result = []
        for face in range(6):
            place = lane + float(128 * face)
            result.append(
                found[face]
                + jnp.where(here == place, there + 1.0, 0.0)
                + jnp.where(there == place, here + 1.0, 0.0)
            )
        return tuple(result)

    found = lax.fori_loop(
        0, LPAIR // 8, find, tuple(jnp.zeros((8, 128), jnp.float32) for _ in range(6))
    )
    partner = [
        jnp.broadcast_to(sublane_sum(value) - 1.0, (16, 128)) for value in found
    ]
    row_id = lax.broadcasted_iota(jnp.int32, (16, 128), 0).astype(jnp.float32)

    def mark(index, carry):
        place = row_id + (index * 16).astype(jnp.float32)
        for face in range(6):
            pairs[pl.ds(pl.multiple_of(index * 16, 16), 16), 128 * face : 128 * face + 128] = (
                jnp.where(partner[face] == place, 1.0, 0.0).astype(jnp.bfloat16)
            )
        return carry

    lax.fori_loop(0, 48, mark, 0)
    lane16 = lax.broadcasted_iota(jnp.int32, (16, 128), 1).astype(jnp.float32)
    for block in range(owners):
        code = columns[2 * LPAIR + 16 * block : 2 * LPAIR + 16 * block + 16, :]
        for face in range(6):
            chosen[16 * block : 16 * block + 16, 128 * face : 128 * face + 128] = jnp.where(
                code == lane16 + float(128 * face), 1.0, 0.0
            ).astype(jnp.bfloat16)

    loads[1].wait()
    volume = jnp.broadcast_to(geometry[0:1, :], (8, 128))
    inverse = [jnp.broadcast_to(geometry[d : d + 1, :], (8, 128)) for d in range(1, 4)]
    squared = [value * value for value in inverse]
    weighted = volume * depth_weight
    for i in range(8):
        for j in range(8):
            mass[64 * i + 8 * j : 64 * i + 8 * j + 8, :] = weighted * (WEIGHTS[i] * WEIGHTS[j])
    loads[2].wait()

    def scale_velocity(index, carry):
        for d in range(3):
            place = rows(index * 8 + d * POINTS)
            velocity[place, :] = velocity[place, :] * inverse[d]
        return carry

    lax.fori_loop(0, 64, scale_velocity, 0, unroll=4)
    loads[3].wait()

    zero = jnp.zeros((8, 128), jnp.float32)

    def sweep(source, base, table, factors, finish):
        def lines(r, carry):
            values = [source[rows(base + 64 * i + 8 * r), :] for i in range(8)]
            moved = product(values, table)
            for i in range(8):
                along_i[rows(64 * i + 8 * r), :] = (
                    values[i] * (1.0 / TIME_STEP) + factors(0, 64 * i + 8 * r) * moved[i]
                )
            values = [source[every_eighth(base + 64 * r + k), :] for k in range(8)]
            moved = product(values, table)
            for k in range(8):
                along_k[every_eighth(64 * r + k), :] = moved[k]
            return carry

        lax.fori_loop(0, 8, lines, 0)

        def close(i, carry):
            values = [source[rows(base + 64 * i + 8 * j), :] for j in range(8)]
            moved = product(values, table)
            for j in range(8):
                place = 64 * i + 8 * j
                total = along_i[rows(place), :] + factors(1, place) * moved[j]
                total = total + factors(2, place) * along_k[rows(place), :]
                carry = finish(place, values[j], mass[rows(place), :] * total, carry)
            return carry

        return lax.fori_loop(0, 8, close, (zero, zero))

    def note(quantity, comp, value):
        partial[pl.ds(quantity * 8 + comp, 1), :] = sublane_sum(value)

    def force(comp, carry):
        base = pl.multiple_of(comp * POINTS, POINTS)

        def finish(place, value, total, sums):
            first[rows(base + place), :] = total
            return sums[0] + total * total, sums[1]

        sums = sweep(
            adjoint,
            base,
            DERIVATIVE_HALVES,
            lambda d, place: velocity[rows(d * POINTS + place), :],
            finish,
        )
        note(0, comp, sums[0])
        return carry

    def kappas(comp):
        kappa = jnp.where(comp == 3, DIFFUSIVITY[3], DIFFUSIVITY[0])
        kappa = jnp.where(comp == 4, DIFFUSIVITY[4], kappa)
        return [kappa * value for value in squared]

    def spread(comp, carry):
        base = pl.multiple_of(comp * POINTS, POINTS)
        scaled = kappas(comp)

        def finish(place, value, total, sums):
            image[rows(base + place), :] = total
            return sums[0] + value * total, sums[1] + total * total

        sums = sweep(first, base, STIFFNESS_HALVES, lambda d, place: scaled[d], finish)
        note(1, comp, sums[0])
        note(2, comp, sums[1])
        return carry

    def energy(comp, carry):
        base = pl.multiple_of(comp * POINTS, POINTS)
        scaled = kappas(comp)

        def finish(place, value, total, sums):
            return sums[0] + value * total, sums[1]

        sums = sweep(image, base, STIFFNESS_HALVES, lambda d, place: scaled[d], finish)
        note(3, comp, sums[0])
        return carry

    def face_copy(turn, step):
        peer = sub_peer(step)
        return pltpu.make_async_remote_copy(
            src_ref=outgoing.at[turn, pl.ds(pl.multiple_of(peer * FMAX, FMAX), FMAX)],
            dst_ref=incoming.at[turn, pl.ds(pl.multiple_of(me * FMAX, FMAX), FMAX)],
            send_sem=face_send.at[turn, step],
            recv_sem=face_recv.at[turn, step],
            device_id={"sub": peer},
            device_id_type=MESH,
        )

    def assemble(turn, field, quantity):
        def gather(comp, carry):
            base = pl.multiple_of(comp * POINTS, POINTS)
            top = pl.multiple_of(comp * FACE_ROWS, 16)
            for face in range(6):
                block = jnp.concatenate(
                    [field[face_slice(face, base, a), :] * inside for a in range(1, 7)], axis=0
                )
                high, low = split(block)
                place = slice(128 * face, 128 * face + 128)
                faces[pl.ds(top, FACE_ROWS), place] = high
                faces[pl.ds(pl.multiple_of(top + HALF_ROWS, 16), FACE_ROWS), place] = low
            return carry

        lax.fori_loop(0, COMP, gather, 0)
        over_lanes = ((1,), (1,))
        outgoing[turn] = dot(chosen[...], faces[0:HALF_ROWS, :], over_lanes) + dot(
            chosen[...], faces[HALF_ROWS:, :], over_lanes
        )
        incoming[turn, pl.ds(pl.multiple_of(me * FMAX, FMAX), FMAX), :] = jnp.zeros(
            (FMAX, HALF_ROWS), jnp.float32
        )
        if turn == 0:
            pl.semaphore_wait(barrier, owners - 1 + n_y - 1 + n_z - 1)
        copies = [face_copy(turn, step) for step in range(1, owners)]
        for copy in copies:
            copy.start()
        plain = ((1,), (0,))
        for part in range(3):
            place = slice(256 * part, 256 * part + 256)
            gained[:, place] = dot(faces[0:HALF_ROWS, :], pairs[:, place], plain) + dot(
                faces[HALF_ROWS:, :], pairs[:, place], plain
            )
        for copy in copies:
            copy.wait_recv()
        arrived = [
            split(jnp.transpose(incoming[turn, :, 128 * part : 128 * part + 128]))
            for part in range(2)
        ]
        for half in range(2):
            strip = slice(128 * half, 128 * half + 128)
            for part in range(3):
                place = slice(256 * part, 256 * part + 256)
                gained[strip, place] = (
                    gained[strip, place]
                    + dot(arrived[half][0], chosen[:, place], plain)
                    + dot(arrived[half][1], chosen[:, place], plain)
                )

        def add(comp, carry):
            base = pl.multiple_of(comp * POINTS, POINTS)
            sums = zero
            for face in range(6):
                for a in range(6):
                    place = face_slice(face, base, a + 1)
                    more = gained[rows(comp * FACE_ROWS + 8 * a), 128 * face : 128 * face + 128]
                    value = field[place, :]
                    sums = sums + value * more
                    field[place, :] = value + more
            here = pl.ds(quantity * 8 + comp, 1)
            partial[here, :] = partial[here, :] + sublane_sum(sums)
            return carry

        lax.fori_loop(0, COMP, add, 0)
        for copy in copies:
            copy.wait_send()

    faces[COMP * FACE_ROWS : HALF_ROWS, :] = jnp.zeros((16, 768), jnp.bfloat16)
    faces[HALF_ROWS + COMP * FACE_ROWS :, :] = jnp.zeros((16, 768), jnp.bfloat16)
    partial[...] = jnp.zeros((32, 128), jnp.float32)

    lax.fori_loop(0, COMP, force, 0)
    assemble(0, first, 0)
    save_first = pltpu.make_async_copy(first, first_hbm, store_sem.at[0])
    save_first.start()
    lax.fori_loop(0, COMP, spread, 0)
    assemble(1, image, 2)
    save_image = pltpu.make_async_copy(image, image_hbm, store_sem.at[1])
    save_image.start()
    lax.fori_loop(0, COMP, energy, 0)

    entry = lax.broadcasted_iota(jnp.int32, (32, 128), 0)
    column = lax.broadcasted_iota(jnp.int32, (32, 128), 1)
    diagonal = entry == column
    whole = jnp.sum(partial[...], axis=1, keepdims=True)
    row = jnp.sum(jnp.where(diagonal, whole, 0.0), axis=0, keepdims=True)

    def total(row, slots, count, mine, peer, target, offset):
        slots[mine] = row
        copies = []
        for step in range(1, count):
            copies.append(
                pltpu.make_async_remote_copy(
                    src_ref=slots.at[mine],
                    dst_ref=slots.at[mine],
                    send_sem=sum_send.at[offset + step],
                    recv_sem=sum_recv.at[offset + step],
                    device_id=target(peer(step)),
                    device_id_type=MESH,
                )
            )
        for copy in copies:
            copy.start()
        for copy in copies:
            copy.wait_recv()
        result = jnp.sum(slots[...], axis=0)
        return result, copies

    row, sent_sub = total(row, sub_slots, owners, me, sub_peer, lambda p: {"sub": p}, 0)
    row, sent_y = total(
        row, y_slots, n_y, my_y, y_peer, lambda p: {"grp": p * n_z + my_z}, owners
    )
    row, sent_z = total(
        row, z_slots, n_z, my_z, z_peer, lambda p: {"grp": my_y * n_z + p}, owners + n_y
    )
    spreaded = jnp.where(diagonal, jnp.broadcast_to(row, (32, 128)), 0.0)
    totals = jnp.broadcast_to(jnp.sum(spreaded, axis=1, keepdims=True), (32, 128))
    bb, bq, qq, qhq = (totals[8 * n : 8 * n + 8] for n in range(4))
    alpha = bb / bq
    scaled_qq = alpha * qq
    norm_next = alpha * scaled_qq - bb
    beta = norm_next / bb
    up = 1.0 + beta
    curve = up * (up * bq - 2.0 * scaled_qq) + alpha * (alpha * qhq)
    alpha_next = norm_next / curve
    factor_ref[0:8, :] = alpha + alpha_next * up
    factor_ref[8:16, :] = -alpha * alpha_next
    for copy in sent_sub + sent_y + sent_z:
        copy.wait_send()
    save_first.wait()
    save_image.wait()


def solution(mesh):
    owners, groups = mesh.shape["sub"], mesh.shape["grp"]
    n_z = 12 if groups % 12 == 0 else max(1, groups // 2)
    n_y = groups // n_z

    def shards(adjoint, velocity, geometry, face_codes):
        elements = adjoint.shape[2]
        flat = COMP * POINTS
        vmem = pltpu.VMEM
        f32, bf16 = jnp.float32, jnp.bfloat16
        anywhere = pl.BlockSpec(memory_space=pl.ANY)
        first, image, factor = pl.pallas_call(
            functools.partial(kernel, (owners, n_y, n_z)),
            out_shape=(
                jax.ShapeDtypeStruct((flat, elements), f32),
                jax.ShapeDtypeStruct((flat, elements), f32),
                jax.ShapeDtypeStruct((16, elements), f32),
            ),
            in_specs=[anywhere] * 4,
            out_specs=(anywhere, anywhere, pl.BlockSpec(memory_space=pltpu.VMEM)),
            scratch_shapes=[
                vmem((flat, elements), f32),
                vmem((3 * POINTS, elements), f32),
                vmem((4, elements), f32),
                vmem((1, 704), jnp.int32),
                vmem((flat, elements), f32),
                vmem((flat, elements), f32),
                vmem((POINTS, elements), f32),
                vmem((POINTS, elements), f32),
                vmem((POINTS, elements), f32),
                vmem((704, 128), f32),
                vmem((768, 768), bf16),
                vmem((128, 768), bf16),
                vmem((2 * HALF_ROWS, 768), bf16),
                vmem((HALF_ROWS, 768), f32),
                vmem((2, 128, HALF_ROWS), f32),
                vmem((2, 128, HALF_ROWS), f32),
                vmem((32, 128), f32),
                vmem((owners, 1, 128), f32),
                vmem((n_y, 1, 128), f32),
                vmem((n_z, 1, 128), f32),
                pltpu.SemaphoreType.DMA((4,)),
                pltpu.SemaphoreType.DMA((2,)),
                pltpu.SemaphoreType.DMA((2, owners)),
                pltpu.SemaphoreType.DMA((2, owners)),
                pltpu.SemaphoreType.DMA((owners + n_y + n_z,)),
                pltpu.SemaphoreType.DMA((owners + n_y + n_z,)),
            ],
            compiler_params=pltpu.CompilerParams(
                collective_id=0, has_side_effects=True, vmem_limit_bytes=32 * 1024 * 1024
            ),
        )(
            adjoint.reshape(flat, elements),
            velocity.reshape(3 * POINTS, elements),
            geometry,
            face_codes,
        )
        shape = (COMP, POINTS, elements)
        return (
            factor[0:COMP, None, :] * first.reshape(shape)
            + factor[8 : 8 + COMP, None, :] * image.reshape(shape)
        )

    placed = (
        P(None, None, ("grp", "sub")),
        P(None, None, ("grp", "sub")),
        P(None, ("grp", "sub")),
        P(("grp", "sub"), None),
    )
    return jax.shard_map(
        shards, mesh=mesh, in_specs=placed, out_specs=P(None, None, ("grp", "sub")), check_vma=False
    )
```

profile of v0, /device:TPU:1, one launch (start us, length us, event | category | flops | bytes accessed | tf_op | source)
XLA Modules:
  0.0 53.9 jit_solution(18064235515957615775)
XLA Ops:
  0.0 0.0 copy-start
  0.0 1.3 %copy-done = f32[5,512,128]{2,1,0:T(8,128)S(1)} copy-done((f32[5,512,128]{2,1,0:T(8,128)S(1)}, f32[5,512,128]{2,1,0:T(8,128)}, u32[]{:S(2)}) %copy-start) | copy-done | bytes 1310744
  1.3 0.0 copy-start.1
  1.3 1.1 %copy-done.1 = f32[3,512,128]{2,1,0:T(8,128)S(1)} copy-done((f32[3,512,128]{2,1,0:T(8,128)S(1)}, f32[3,512,128]{2,1,0:T(8,128)}, u32[]{:S(2)}) %copy-start.1) | copy-done | bytes 786456
  2.5 0.0 copy-start.2
  2.5 0.7 %copy-done.2 = s32[1,704]{1,0:T(1,128)S(1)} copy-done((s32[1,704]{1,0:T(1,128)S(1)}, s32[1,704]{1,0:T(1,128)}, u32[]{:S(2)}) %copy-start.2) | copy-done | bytes 2840
  3.1 0.0 copy-start.3
  3.1 0.7 %copy-done.3 = f32[4,128]{1,0:T(4,128)S(1)} copy-done((f32[4,128]{1,0:T(4,128)S(1)}, f32[4,128]{1,0:T(4,128)}, u32[]{:S(2)}) %copy-start.3) | copy-done | bytes 2072
  3.8 48.9 %shard_map.46 = (f32[2560,128]{1,0:T(8,128)S(1)}, f32[2560,128]{1,0:T(8,128)S(1)}, f32[16,128]{1,0:T(8,128)S(1)}) custom-call(f32[2560,128]{1,0:T(8,128)S(1)} %bitcast.4, f32[1536,128]{1,0:T(8,128)S(1)} %bitcast.7, f32[4,128]{1,0:T(4,128)S(1)} %copy-done.3, s32[1,704]{1,0:T(1,128)S(1)} %copy-done.2), custom_call_target="tpu_custom_call" | custom-call | tf_op jit(solution)/shard_map/pallas_call | solution.py:502
  52.7 1.2 %multiply_add_fusion = f32[5,512,128]{2,1,0:T(8,128)} fusion(f32[5,512,128]{2,1,0:T(8,128)S(1)} %bitcast.6, f32[5,512,128]{2,1,0:T(8,128)S(1)} %bitcast.5, f32[5,128]{1,0:T(8,128)S(1)} %get-tuple-element.12, f32[5,128]{1,0:T(8,128)S(1)} %get-tuple-element.11), kind=kLoop, calls=%fused_computation | loop fusion | flops 983040 | bytes 3937280 | tf_op jit(solution)/shard_map/add | solution.py:550
  (1 shorter events, 0.0 us)
Async XLA Ops:
  0.0 1.3 %copy-start = (f32[5,512,128]{2,1,0:T(8,128)S(1)}, f32[5,512,128]{2,1,0:T(8,128)}, u32[]{:S(2)}) copy-start(f32[5,512,128]{2,1,0:T(8,128)} %param.4) | copy-start | bytes 3932164
  1.3 1.1 %copy-start.1 = (f32[3,512,128]{2,1,0:T(8,128)S(1)}, f32[3,512,128]{2,1,0:T(8,128)}, u32[]{:S(2)}) copy-start(f32[3,512,128]{2,1,0:T(8,128)} %param.5) | copy-start | bytes 2359300
  2.5 0.7 %copy-start.2 = (s32[1,704]{1,0:T(1,128)S(1)}, s32[1,704]{1,0:T(1,128)}, u32[]{:S(2)}) copy-start(s32[1,704]{1,0:T(1,128)} %codes_hbm.1) | copy-start | bytes 8452
  3.1 0.7 %copy-start.3 = (f32[4,128]{1,0:T(4,128)S(1)}, f32[4,128]{1,0:T(4,128)}, u32[]{:S(2)}) copy-start(f32[4,128]{1,0:T(4,128)} %geometry_hbm.1) | copy-start | bytes 6148
where the time goes:
time: 54.2 us; the launch traced here: 53.9 us
  Pallas kernels  48.9 us (90%)
  local copies, waits for them, and re-layouts  3.82 us (7%)
  other arithmetic  1.2 us (2%)
    pallas_call x1, Pallas kernels, shards(): pl.pallas_call(functools.partial(kernel, (owners, n_y, n_z)), out_shape=(...  48.9 us
    unnamed x8, local copies, waits for them, and re-layouts  3.81 us
    add x1, other arithmetic, shards(): factor[0:COMP, None, :] * first.reshape(shape)  1.2 us

commit v1 on v0

v1 whole, which is shorter than its diff:
```python
import functools

import jax
import jax.numpy as jnp
from jax import lax
from jax.experimental import pallas as pl
from jax.experimental.pallas import tpu as pltpu
from jax.sharding import PartitionSpec as P

MESH = pl.DeviceIdType.MESH
COMP = 5
POINTS = 512
LPAIR = 288
FMAX = 16
FACE_ROWS = 48
HALF_ROWS = 256
TIME_STEP = 0.05
DIFFUSIVITY = (1.0, 1.0, 1.0, 0.7, 0.2)
GLL_POINTS = (
    -1.0,
    -0.8717401485096066,
    -0.5917001814331423,
    -0.2092992179024789,
    0.2092992179024789,
    0.5917001814331423,
    0.8717401485096066,
    1.0,
)


def legendre_seven(point):
    before = 1.0
    current = point
    for order in range(1, 7):
        following = ((2 * order + 1) * point * current - order * before) / (order + 1)
        before = current
        current = following
    return current


def gll_tables():
    points = list(GLL_POINTS)
    values = [legendre_seven(point) for point in points]
    weights = [2.0 / (56.0 * value * value) for value in values]
    derivative = []
    for row in range(8):
        line = []
        for col in range(8):
            if row == col:
                line.append(0.0)
            else:
                line.append(values[row] / (values[col] * (points[row] - points[col])))
        derivative.append(line)
    derivative[0][0] = -14.0
    derivative[7][7] = 14.0
    stiffness = []
    for row in range(8):
        line = []
        for col in range(8):
            total = 0.0
            for mid in range(8):
                total += derivative[mid][row] * weights[mid] * derivative[mid][col]
            line.append(total / weights[row])
        stiffness.append(line)
    return weights, derivative, stiffness


def halves(matrix):
    even = [[0.5 * (matrix[i][a] + matrix[i][7 - a]) for a in range(4)] for i in range(4)]
    odd = [[0.5 * (matrix[i][a] - matrix[i][7 - a]) for a in range(4)] for i in range(4)]
    return even, odd


def triangle(matrix):
    result = [[0.0] * 4 for _ in range(4)]
    for r in range(4):
        pivot = matrix[r][r] - sum(result[m][r] ** 2 for m in range(r))
        if pivot < 1e-9 * matrix[r][r]:
            continue
        result[r][r] = pivot**0.5
        for c in range(r + 1, 4):
            rest = matrix[r][c] - sum(result[m][r] * result[m][c] for m in range(r))
            result[r][c] = rest / result[r][r]
    return result


WEIGHTS, DERIVATIVE, STIFFNESS = gll_tables()
SYMMETRIC_HALVES = halves([[WEIGHTS[i] * v for v in STIFFNESS[i]] for i in range(8)])
SQUARES = tuple(triangle(part) for part in SYMMETRIC_HALVES)
GROUPS = ((0, 2), (2, 4), (4, 5))
DERIVATIVE_HALVES = halves(DERIVATIVE) + (-1,)
STIFFNESS_HALVES = halves(STIFFNESS) + (1,)


def product(values, table):
    even, odd, sign = table
    sums = [values[a] + values[7 - a] for a in range(4)]
    gaps = [values[a] - values[7 - a] for a in range(4)]
    result = [None] * 8
    for i in range(4):
        first = sum(even[i][a] * sums[a] for a in range(1, 4)) + even[i][0] * sums[0]
        second = sum(odd[i][a] * gaps[a] for a in range(1, 4)) + odd[i][0] * gaps[0]
        result[i] = first + second
        result[7 - i] = first - second if sign > 0 else second - first
    return result


def quadratic(values):
    sums = [values[a] + values[7 - a] for a in range(4)]
    gaps = [values[a] - values[7 - a] for a in range(4)]
    result = None
    for table, part in zip(SQUARES, (sums, gaps)):
        for r in range(4):
            if table[r][r] == 0.0:
                continue
            term = table[r][r] * part[r]
            for c in range(r + 1, 4):
                term = term + table[r][c] * part[c]
            term = term * term
            result = term if result is None else result + term
    return result


def rows(start):
    return pl.ds(pl.multiple_of(start, 8), 8)


def every_eighth(start):
    return pl.ds(start, 8, stride=8)


def sublane_sum(value):
    return jnp.sum(value, axis=0, keepdims=True)


def split(value):
    high = value.astype(jnp.bfloat16)
    low = (value - high.astype(jnp.float32)).astype(jnp.bfloat16)
    return high, low


def dot(first, second, dims):
    return lax.dot_general(
        first, second, (dims, ((), ())), preferred_element_type=jnp.float32
    )


def face_slice(face, base, step):
    direction, level = face // 2, 7 * (face % 2)
    if direction == 0:
        return pl.ds(pl.multiple_of(base + 64 * level + 8 * step, 8), 8)
    if direction == 1:
        return pl.ds(pl.multiple_of(base + 64 * step + 8 * level, 8), 8)
    return pl.ds(base + 64 * step + level, 8, stride=8)


def kernel(
    sizes,
    adjoint_hbm,
    velocity_hbm,
    geometry_hbm,
    codes_hbm,
    first,
    image,
    factor_ref,
    adjoint,
    velocity,
    geometry,
    codes,
    mass,
    along_i,
    along_k,
    columns,
    pairs,
    chosen,
    faces,
    gained,
    outgoing,
    incoming,
    partial,
    near_slots,
    far_slots,
    load_sem,
    face_send,
    face_recv,
    near_send,
    near_recv,
    far_send,
    far_recv,
):
    owners, n_y, n_z = sizes
    n_x = owners // 2
    me = lax.axis_index("sub")
    group = lax.axis_index("grp")
    my_y = group // n_z
    my_z = group - my_y * n_z
    my_x = me // 2
    my_core = me - my_x * 2

    def load(index, source, target):
        return pltpu.make_async_copy(source, target, load_sem.at[index])

    loads = [load(0, codes_hbm, codes), load(1, geometry_hbm, geometry)]
    loads.append(load(2, velocity_hbm, velocity))
    for index, (low, high) in enumerate(GROUPS):
        part = pl.ds(low * POINTS, (high - low) * POINTS)
        loads.append(load(3 + index, adjoint_hbm.at[part], adjoint.at[part]))
    for copy in loads:
        copy.start()

    barrier = pltpu.get_barrier_semaphore()
    n_near, n_far = 2 * n_z, n_x * n_y
    near_me = my_z * 2 + my_core
    far_me = my_y * n_x + my_x

    def sub_peer(step):
        return {"grp": group, "sub": lax.rem(me + step, owners)}

    def near_peer(step):
        place = lax.rem(near_me + step, n_near)
        z = place // 2
        return {"grp": my_y * n_z + z, "sub": my_x * 2 + (place - z * 2)}

    def far_peer(step):
        place = lax.rem(far_me + step, n_far)
        y = place // n_x
        return {"grp": y * n_z + my_z, "sub": (place - y * n_x) * 2 + my_core}

    for count, peer in ((owners, sub_peer), (n_near, near_peer), (n_far, far_peer)):

        def greet(step, carry, peer=peer):
            pl.semaphore_signal(barrier, inc=1, device_id=peer(step), device_id_type=MESH)
            return carry

        lax.fori_loop(1, count, greet, 0)

    sublane = lax.broadcasted_iota(jnp.int32, (8, 128), 0)
    lane = lax.broadcasted_iota(jnp.int32, (8, 128), 1).astype(jnp.float32)
    inside = jnp.where((sublane >= 1) & (sublane <= 6), 1.0, 0.0)
    depth_weight = jnp.zeros((8, 128), jnp.float32)
    for k in range(8):
        depth_weight = jnp.where(sublane == k, WEIGHTS[k], depth_weight)
    zero = jnp.zeros((8, 128), jnp.float32)

    loads[0].wait()
    for tile in range(6):
        width = min(128, 704 - 128 * tile)
        row = codes[:, 128 * tile : 128 * tile + width].astype(jnp.float32)
        columns[128 * tile : 128 * tile + width, :] = jnp.transpose(
            jnp.broadcast_to(row, (128, width))
        )
    lane16 = lax.broadcasted_iota(jnp.int32, (16, 128), 1).astype(jnp.float32)
    for block in range(owners):
        code = columns[2 * LPAIR + 16 * block : 2 * LPAIR + 16 * block + 16, :]
        for face in range(6):
            chosen[16 * block : 16 * block + 16, 128 * face : 128 * face + 128] = jnp.where(
                code == lane16 + float(128 * face), 1.0, 0.0
            ).astype(jnp.bfloat16)
    for turn in range(2):
        own = pl.ds(pl.multiple_of(me * FMAX, FMAX), FMAX)
        for index in range(len(GROUPS)):
            outgoing[turn, index, :, 96:128] = jnp.zeros((128, 32), jnp.float32)
            incoming[turn, index, own, :] = jnp.zeros((FMAX, 128), jnp.float32)
    outgoing[:, 2, :, 0:128] = jnp.zeros((2, 128, 128), jnp.float32)

    loads[1].wait()
    volume = jnp.broadcast_to(geometry[0:1, :], (8, 128))
    inverse = [jnp.broadcast_to(geometry[d : d + 1, :], (8, 128)) for d in range(1, 4)]
    squared = [value * value for value in inverse]
    weighted = volume * depth_weight
    for i in range(8):
        for j in range(8):
            mass[64 * i + 8 * j : 64 * i + 8 * j + 8, :] = weighted * (WEIGHTS[i] * WEIGHTS[j])
    loads[2].wait()

    def scale_velocity(index, carry):
        for d in range(3):
            place = rows(index * 8 + d * POINTS)
            velocity[place, :] = velocity[place, :] * inverse[d]
        return carry

    lax.fori_loop(0, 64, scale_velocity, 0, unroll=4)

    def build_pairs():
        def find(index, found):
            here = columns[rows(index * 8), :]
            there = columns[rows(index * 8 + LPAIR), :]
            result = []
            for face in range(6):
                place = lane + float(128 * face)
                result.append(
                    found[face]
                    + jnp.where(here == place, there + 1.0, 0.0)
                    + jnp.where(there == place, here + 1.0, 0.0)
                )
            return tuple(result)

        found = lax.fori_loop(0, LPAIR // 8, find, (zero,) * 6, unroll=4)
        partner = [jnp.broadcast_to(sublane_sum(value) - 1.0, (16, 128)) for value in found]
        row_id = lax.broadcasted_iota(jnp.int32, (16, 128), 0).astype(jnp.float32)

        def mark(index, carry):
            place = row_id + (index * 16).astype(jnp.float32)
            here = pl.ds(pl.multiple_of(index * 16, 16), 16)
            for face in range(6):
                pairs[here, 128 * face : 128 * face + 128] = jnp.where(
                    partner[face] == place, 1.0, 0.0
                ).astype(jnp.bfloat16)
            return carry

        lax.fori_loop(0, 48, mark, 0, unroll=2)

    def sweep(source, base, table, factors, finish):
        def lines(r, carry):
            values = [source[rows(base + 64 * i + 8 * r), :] for i in range(8)]
            moved = product(values, table)
            for i in range(8):
                along_i[rows(64 * i + 8 * r), :] = (
                    values[i] * (1.0 / TIME_STEP) + factors(0, 64 * i + 8 * r) * moved[i]
                )
            values = [source[every_eighth(base + 64 * r + k), :] for k in range(8)]
            moved = product(values, table)
            for k in range(8):
                along_k[every_eighth(64 * r + k), :] = moved[k]
            return carry

        lax.fori_loop(0, 8, lines, 0)

        def close(i, carry):
            values = [source[rows(base + 64 * i + 8 * j), :] for j in range(8)]
            moved = product(values, table)
            for j in range(8):
                place = 64 * i + 8 * j
                total = along_i[rows(place), :] + factors(1, place) * moved[j]
                total = total + factors(2, place) * along_k[rows(place), :]
                carry = finish(place, values[j], mass[rows(place), :] * total, carry)
            return carry

        return lax.fori_loop(0, 8, close, (zero, zero))

    def note(quantity, comp, value):
        partial[pl.ds(quantity * 8 + comp, 1), :] = sublane_sum(value)

    def force(comp, carry):
        base = pl.multiple_of(comp * POINTS, POINTS)

        def finish(place, value, total, sums):
            first[rows(base + place), :] = total
            return sums[0] + total * total, sums[1]

        sums = sweep(
            adjoint,
            base,
            DERIVATIVE_HALVES,
            lambda d, place: velocity[rows(d * POINTS + place), :],
            finish,
        )
        note(0, comp, sums[0])
        return carry

    def kappas(comp):
        kappa = jnp.where(comp == 3, DIFFUSIVITY[3], DIFFUSIVITY[0])
        kappa = jnp.where(comp == 4, DIFFUSIVITY[4], kappa)
        return [kappa * value for value in squared]

    def spread(comp, carry):
        base = pl.multiple_of(comp * POINTS, POINTS)
        scaled = kappas(comp)

        def finish(place, value, total, sums):
            image[rows(base + place), :] = total
            return sums[0] + value * total, sums[1] + total * total

        sums = sweep(first, base, STIFFNESS_HALVES, lambda d, place: scaled[d], finish)
        note(1, comp, sums[0])
        note(2, comp, sums[1])
        return carry

    def energy(comp, carry):
        base = pl.multiple_of(comp * POINTS, POINTS)
        scaled = kappas(comp)
        forms = [zero, zero, zero]
        plain = zero
        for r in range(8):
            lines_i = [image[rows(base + 64 * i + 8 * r), :] for i in range(8)]
            forms[0] = forms[0] + WEIGHTS[r] * quadratic(lines_i)
            lines_j = [image[rows(base + 64 * r + 8 * j), :] for j in range(8)]
            forms[1] = forms[1] + WEIGHTS[r] * quadratic(lines_j)
            lines_k = [image[every_eighth(base + 64 * r + k), :] for k in range(8)]
            forms[2] = forms[2] + WEIGHTS[r] * quadratic(lines_k)
            level = [lines_j[j] * lines_j[j] for j in range(8)]
            level = sum((WEIGHTS[j] * (level[j] + level[7 - j]) for j in range(1, 4)), WEIGHTS[0] * (level[0] + level[7]))
            plain = plain + WEIGHTS[r] * level
        total = plain * (1.0 / TIME_STEP)
        for d in range(3):
            total = total + scaled[d] * forms[d]
        note(3, comp, weighted * total)
        return carry

    def face_copy(turn, index, step):
        peer = sub_peer(step)
        return pltpu.make_async_remote_copy(
            src_ref=outgoing.at[turn, index, pl.ds(pl.multiple_of(peer["sub"] * FMAX, FMAX), FMAX)],
            dst_ref=incoming.at[turn, index, pl.ds(pl.multiple_of(me * FMAX, FMAX), FMAX)],
            send_sem=face_send.at[turn, index, step],
            recv_sem=face_recv.at[turn, index, step],
            device_id=peer,
            device_id_type=MESH,
        )

    def each_copy(turn, index, act):
        def one(step, carry):
            act(face_copy(turn, index, step))
            return carry

        lax.fori_loop(1, owners, one, 0)

    def send(turn, index, field):
        low, high = GROUPS[index]

        def gather(comp, carry):
            base = pl.multiple_of(comp * POINTS, POINTS)
            top = pl.multiple_of(comp * FACE_ROWS, 16)
            for face in range(6):
                block = jnp.concatenate(
                    [field[face_slice(face, base, a), :] * inside for a in range(1, 7)], axis=0
                )
                big, small = split(block)
                place = slice(128 * face, 128 * face + 128)
                faces[pl.ds(top, FACE_ROWS), place] = big
                faces[pl.ds(pl.multiple_of(top + HALF_ROWS, 16), FACE_ROWS), place] = small
            return carry

        lax.fori_loop(low, high, gather, 0)
        start, stop = low * FACE_ROWS, high * FACE_ROWS
        over_lanes = ((1,), (1,))
        outgoing[turn, index, :, 0 : stop - start] = dot(
            chosen[...], faces[start:stop, :], over_lanes
        ) + dot(chosen[...], faces[HALF_ROWS + start : HALF_ROWS + stop, :], over_lanes)
        if turn == 0 and index == 0:
            pl.semaphore_wait(barrier, owners - 1 + n_near - 1 + n_far - 1)
        each_copy(turn, index, lambda copy: copy.start())

    plain_dims = ((1,), (0,))

    def local():
        for part in range(3):
            place = slice(256 * part, 256 * part + 256)
            gained[:, place] = dot(faces[0:HALF_ROWS, :], pairs[:, place], plain_dims) + dot(
                faces[HALF_ROWS:, :], pairs[:, place], plain_dims
            )

    def receive(turn, index, field, quantity):
        low, high = GROUPS[index]
        start, stop = low * FACE_ROWS, high * FACE_ROWS
        each_copy(turn, index, lambda copy: copy.wait_recv())
        big, small = split(jnp.transpose(incoming[turn, index])[0 : stop - start, :])
        for part in range(3):
            place = slice(256 * part, 256 * part + 256)
            gained[start:stop, place] = (
                gained[start:stop, place]
                + dot(big, chosen[:, place], plain_dims)
                + dot(small, chosen[:, place], plain_dims)
            )

        def add(comp, carry):
            base = pl.multiple_of(comp * POINTS, POINTS)
            sums = zero
            for face in range(6):
                for a in range(6):
                    place = face_slice(face, base, a + 1)
                    more = gained[rows(comp * FACE_ROWS + 8 * a), 128 * face : 128 * face + 128]
                    value = field[place, :]
                    sums = sums + value * more
                    field[place, :] = value + more
            here = pl.ds(quantity * 8 + comp, 1)
            partial[here, :] = partial[here, :] + sublane_sum(sums)
            return carry

        lax.fori_loop(low, high, add, 0)

    faces[COMP * FACE_ROWS : HALF_ROWS, :] = jnp.zeros((16, 768), jnp.bfloat16)
    faces[HALF_ROWS + COMP * FACE_ROWS :, :] = jnp.zeros((16, 768), jnp.bfloat16)
    partial[...] = jnp.zeros((32, 128), jnp.float32)

    for index, (low, high) in enumerate(GROUPS):
        loads[3 + index].wait()
        lax.fori_loop(low, high, force, 0)
        send(0, index, first)
    build_pairs()
    local()
    for index, (low, high) in enumerate(GROUPS):
        receive(0, index, first, 0)
        lax.fori_loop(low, high, spread, 0)
        send(1, index, image)
    local()
    for index, (low, high) in enumerate(GROUPS):
        receive(1, index, image, 2)
        lax.fori_loop(low, high, energy, 0)

    entry = lax.broadcasted_iota(jnp.int32, (32, 128), 0)
    column = lax.broadcasted_iota(jnp.int32, (32, 128), 1)
    diagonal = entry == column
    whole = jnp.sum(partial[...], axis=1, keepdims=True)
    row = jnp.sum(jnp.where(diagonal, whole, 0.0), axis=0, keepdims=True)

    def sum_copy(slots, mine, peer, send_sems, recv_sems, step):
        return pltpu.make_async_remote_copy(
            src_ref=slots.at[mine],
            dst_ref=slots.at[mine],
            send_sem=send_sems.at[step],
            recv_sem=recv_sems.at[step],
            device_id=peer(step),
            device_id_type=MESH,
        )

    stages = (
        (near_slots, n_near, near_me, near_peer, near_send, near_recv),
        (far_slots, n_far, far_me, far_peer, far_send, far_recv),
    )
    for slots, count, mine, peer, send_sems, recv_sems in stages:
        slots[mine] = row

        def begin(step, carry, given=(slots, mine, peer, send_sems, recv_sems)):
            sum_copy(*given, step).start()
            return carry

        def arrive(step, carry, given=(slots, mine, peer, send_sems, recv_sems)):
            sum_copy(*given, step).wait_recv()
            return carry

        lax.fori_loop(1, count, begin, 0)
        lax.fori_loop(1, count, arrive, 0)
        row = jnp.sum(slots[...], axis=0)

    spreaded = jnp.where(diagonal, jnp.broadcast_to(row, (32, 128)), 0.0)
    totals = jnp.broadcast_to(jnp.sum(spreaded, axis=1, keepdims=True), (32, 128))
    bb, bq, qq, qhq = (totals[8 * n : 8 * n + 8] for n in range(4))
    alpha = bb / bq
    scaled_qq = alpha * qq
    norm_next = alpha * scaled_qq - bb
    beta = norm_next / bb
    up = 1.0 + beta
    curve = up * (up * bq - 2.0 * scaled_qq) + alpha * (alpha * qhq)
    alpha_next = norm_next / curve
    factor_ref[0:8, :] = alpha + alpha_next * up
    factor_ref[8:16, :] = -alpha * alpha_next

    for turn in range(2):
        for index in range(len(GROUPS)):
            each_copy(turn, index, lambda copy: copy.wait_send())
    for slots, count, mine, peer, send_sems, recv_sems in stages:

        def leave(step, carry, given=(slots, mine, peer, send_sems, recv_sems)):
            sum_copy(*given, step).wait_send()
            return carry

        lax.fori_loop(1, count, leave, 0)


def solution(mesh):
    owners, groups = mesh.shape["sub"], mesh.shape["grp"]
    n_z = 12 if groups % 12 == 0 else max(1, groups // 2)
    n_y = groups // n_z

    def shards(adjoint, velocity, geometry, face_codes):
        elements = adjoint.shape[2]
        flat = COMP * POINTS
        vmem = pltpu.VMEM
        f32, bf16 = jnp.float32, jnp.bfloat16
        hbm = pl.BlockSpec(memory_space=pltpu.HBM)

        def keep(array):
            return pltpu.with_memory_space_constraint(array, pltpu.HBM)

        inner = pl.BlockSpec(memory_space=pltpu.VMEM)
        n_near, n_far = 2 * n_z, n_y * owners // 2
        dma = pltpu.SemaphoreType.DMA
        first, image, factor = pl.pallas_call(
            functools.partial(kernel, (owners, n_y, n_z)),
            out_shape=(
                pltpu.VMEM((flat, elements), f32),
                pltpu.VMEM((flat, elements), f32),
                pltpu.VMEM((16, elements), f32),
            ),
            in_specs=[hbm] * 4,
            out_specs=(inner, inner, inner),
            scratch_shapes=[
                vmem((flat, elements), f32),
                vmem((3 * POINTS, elements), f32),
                vmem((4, elements), f32),
                vmem((1, 704), jnp.int32),
                vmem((POINTS, elements), f32),
                vmem((POINTS, elements), f32),
                vmem((POINTS, elements), f32),
                vmem((704, 128), f32),
                vmem((768, 768), bf16),
                vmem((128, 768), bf16),
                vmem((2 * HALF_ROWS, 768), bf16),
                vmem((HALF_ROWS, 768), f32),
                vmem((2, len(GROUPS), 128, 128), f32),
                vmem((2, len(GROUPS), 128, 128), f32),
                vmem((32, 128), f32),
                vmem((n_near, 1, 128), f32),
                vmem((n_far, 1, 128), f32),
                dma((3 + len(GROUPS),)),
                dma((2, len(GROUPS), owners)),
                dma((2, len(GROUPS), owners)),
                dma((n_near,)),
                dma((n_near,)),
                dma((n_far,)),
                dma((n_far,)),
            ],
            compiler_params=pltpu.CompilerParams(
                collective_id=0, has_side_effects=True, vmem_limit_bytes=32 * 1024 * 1024
            ),
        )(
            keep(adjoint.reshape(flat, elements)),
            keep(velocity.reshape(3 * POINTS, elements)),
            keep(geometry),
            keep(face_codes),
        )
        shape = (COMP, POINTS, elements)
        return (
            factor[0:COMP, None, :] * first.reshape(shape)
            + factor[8 : 8 + COMP, None, :] * image.reshape(shape)
        )

    placed = (
        P(None, None, ("grp", "sub")),
        P(None, None, ("grp", "sub")),
        P(None, ("grp", "sub")),
        P(("grp", "sub"), None),
    )
    return jax.shard_map(
        shards, mesh=mesh, in_specs=placed, out_specs=P(None, None, ("grp", "sub")), check_vma=False
    )
```

time: 54.2 us -> 48.9 us (0.902)
  local copies, waits for them, and re-layouts: 3.82 us -> 0.01 us
  Pallas kernels: 48.9 us -> 47.5 us
    unnamed x8 -> x0, local copies, waits for them, and re-layouts: 3.81 us -> none
    pallas_call x1, Pallas kernels: 48.9 us -> 47.5 us  [shards(): pl.pallas_call(functools.partial(kernel, (owners, n_y, n_z)), out_shape=(...]
where the time goes in v1:
time: 48.9 us; the launch traced here: 48.7 us
  Pallas kernels  47.5 us (97%)
  other arithmetic  1.2 us (2%)
    pallas_call x1, Pallas kernels, shards(): pl.pallas_call(functools.partial(kernel, (owners, n_y, n_z)), out_shape=(...  47.5 us
    add x1, other arithmetic, shards(): factor[0:COMP, None, :] * first.reshape(shape)  1.2 us

profile of v1, /device:TPU:1, one launch (start us, length us, event | category | flops | bytes accessed | tf_op | source)
XLA Modules:
  0.0 48.7 jit_solution(15780427316150947425)
XLA Ops:
  0.0 47.5 %shard_map.46 = (f32[2560,128]{1,0:T(8,128)S(1)}, f32[2560,128]{1,0:T(8,128)S(1)}, f32[16,128]{1,0:T(8,128)S(1)}) custom-call(f32[2560,128]{1,0:T(8,128)} %bitcast.6, f32[1536,128]{1,0:T(8,128)} %bitcast.7, f32[4,128]{1,0:T(4,128)} %geometry_hbm.1, s32[1,704]{1,0:T(1,128)} %codes_hbm.1), custom_call_target="tpu_custom_call" | custom-call | tf_op jit(solution)/shard_map/pallas_call | solution.py:579
  47.5 1.2 %multiply_add_fusion = f32[5,512,128]{2,1,0:T(8,128)} fusion(f32[5,512,128]{2,1,0:T(8,128)S(1)} %bitcast.5, f32[5,512,128]{2,1,0:T(8,128)S(1)} %bitcast.4, f32[5,128]{1,0:T(8,128)S(1)} %get-tuple-element.12, f32[5,128]{1,0:T(8,128)S(1)} %get-tuple-element.11), kind=kLoop, calls=%fused_computation | loop fusion | flops 983040 | bytes 3937280 | tf_op jit(solution)/shard_map/add | solution.py:625
  (1 shorter events, 0.0 us)

commit v2 on v1

--- a/solution.py
+++ b/solution.py
@@ -127,6 +127,10 @@
 
 def every_eighth(start):
     return pl.ds(start, 8, stride=8)
+
+
+def far_first(count):
+    return sorted(range(1, count), key=lambda step: (abs(2 * step - count), step))
 
 
 def sublane_sum(value):
@@ -232,7 +236,7 @@
             pl.semaphore_signal(barrier, inc=1, device_id=peer(step), device_id_type=MESH)
             return carry
 
-        lax.fori_loop(1, count, greet, 0)
+        lax.fori_loop(1, count, greet, 0, unroll=4)
 
     sublane = lax.broadcasted_iota(jnp.int32, (8, 128), 0)
     lane = lax.broadcasted_iota(jnp.int32, (8, 128), 1).astype(jnp.float32)
@@ -259,9 +263,8 @@
     for turn in range(2):
         own = pl.ds(pl.multiple_of(me * FMAX, FMAX), FMAX)
         for index in range(len(GROUPS)):
-            outgoing[turn, index, :, 96:128] = jnp.zeros((128, 32), jnp.float32)
+            outgoing[turn, index] = jnp.zeros((128, 128), jnp.float32)
             incoming[turn, index, own, :] = jnp.zeros((FMAX, 128), jnp.float32)
-    outgoing[:, 2, :, 0:128] = jnp.zeros((2, 128, 128), jnp.float32)
 
     loads[1].wait()
     volume = jnp.broadcast_to(geometry[0:1, :], (8, 128))
@@ -288,15 +291,14 @@
             result = []
             for face in range(6):
                 place = lane + float(128 * face)
-                result.append(
-                    found[face]
-                    + jnp.where(here == place, there + 1.0, 0.0)
-                    + jnp.where(there == place, here + 1.0, 0.0)
-                )
+                value = jnp.where(here == place, there, found[face])
+                result.append(jnp.where(there == place, here, value))
             return tuple(result)
 
-        found = lax.fori_loop(0, LPAIR // 8, find, (zero,) * 6, unroll=4)
-        partner = [jnp.broadcast_to(sublane_sum(value) - 1.0, (16, 128)) for value in found]
+        found = lax.fori_loop(0, LPAIR // 8, find, (zero - 1.0,) * 6, unroll=4)
+        partner = [
+            jnp.broadcast_to(jnp.max(value, axis=0, keepdims=True), (16, 128)) for value in found
+        ]
         row_id = lax.broadcasted_iota(jnp.int32, (16, 128), 0).astype(jnp.float32)
 
         def mark(index, carry):
@@ -308,7 +310,7 @@
                 ).astype(jnp.bfloat16)
             return carry
 
-        lax.fori_loop(0, 48, mark, 0, unroll=2)
+        lax.fori_loop(0, 48, mark, 0, unroll=8)
 
     def sweep(source, base, table, factors, finish):
         def lines(r, carry):
@@ -324,7 +326,7 @@
                 along_k[every_eighth(64 * r + k), :] = moved[k]
             return carry
 
-        lax.fori_loop(0, 8, lines, 0)
+        lax.fori_loop(0, 8, lines, 0, unroll=True)
 
         def close(i, carry):
             values = [source[rows(base + 64 * i + 8 * j), :] for j in range(8)]
@@ -336,7 +338,7 @@
                 carry = finish(place, values[j], mass[rows(place), :] * total, carry)
             return carry
 
-        return lax.fori_loop(0, 8, close, (zero, zero))
+        return lax.fori_loop(0, 8, close, (zero, zero), unroll=True)
 
     def note(quantity, comp, value):
         partial[pl.ds(quantity * 8 + comp, 1), :] = sublane_sum(value)
@@ -409,11 +411,8 @@
         )
 
     def each_copy(turn, index, act):
-        def one(step, carry):
+        for step in far_first(owners):
             act(face_copy(turn, index, step))
-            return carry
-
-        lax.fori_loop(1, owners, one, 0)
 
     def send(turn, index, field):
         low, high = GROUPS[index]
@@ -431,7 +430,7 @@
                 faces[pl.ds(pl.multiple_of(top + HALF_ROWS, 16), FACE_ROWS), place] = small
             return carry
 
-        lax.fori_loop(low, high, gather, 0)
+        lax.fori_loop(low, high, gather, 0, unroll=True)
         start, stop = low * FACE_ROWS, high * FACE_ROWS
         over_lanes = ((1,), (1,))
         outgoing[turn, index, :, 0 : stop - start] = dot(
@@ -465,19 +464,22 @@
 
         def add(comp, carry):
             base = pl.multiple_of(comp * POINTS, POINTS)
+            places = [face_slice(face, base, a + 1) for face in range(6) for a in range(6)]
+            values = [field[place, :] for place in places]
+            extra = [
+                gained[rows(comp * FACE_ROWS + 8 * a), 128 * face : 128 * face + 128]
+                for face in range(6)
+                for a in range(6)
+            ]
             sums = zero
-            for face in range(6):
-                for a in range(6):
-                    place = face_slice(face, base, a + 1)
-                    more = gained[rows(comp * FACE_ROWS + 8 * a), 128 * face : 128 * face + 128]
-                    value = field[place, :]
-                    sums = sums + value * more
-                    field[place, :] = value + more
+            for place, value, more in zip(places, values, extra):
+                sums = sums + value * more
+                field[place, :] = value + more
             here = pl.ds(quantity * 8 + comp, 1)
             partial[here, :] = partial[here, :] + sublane_sum(sums)
             return carry
 
-        lax.fori_loop(low, high, add, 0)
+        lax.fori_loop(low, high, add, 0, unroll=True)
 
     faces[COMP * FACE_ROWS : HALF_ROWS, :] = jnp.zeros((16, 768), jnp.bfloat16)
     faces[HALF_ROWS + COMP * FACE_ROWS :, :] = jnp.zeros((16, 768), jnp.bfloat16)
@@ -485,18 +487,18 @@
 
     for index, (low, high) in enumerate(GROUPS):
         loads[3 + index].wait()
-        lax.fori_loop(low, high, force, 0)
+        lax.fori_loop(low, high, force, 0, unroll=True)
         send(0, index, first)
     build_pairs()
     local()
     for index, (low, high) in enumerate(GROUPS):
         receive(0, index, first, 0)
-        lax.fori_loop(low, high, spread, 0)
+        lax.fori_loop(low, high, spread, 0, unroll=True)
         send(1, index, image)
     local()
     for index, (low, high) in enumerate(GROUPS):
         receive(1, index, image, 2)
-        lax.fori_loop(low, high, energy, 0)
+        lax.fori_loop(low, high, energy, 0, unroll=True)
 
     entry = lax.broadcasted_iota(jnp.int32, (32, 128), 0)
     column = lax.broadcasted_iota(jnp.int32, (32, 128), 1)
@@ -521,16 +523,10 @@
     for slots, count, mine, peer, send_sems, recv_sems in stages:
         slots[mine] = row
 
-        def begin(step, carry, given=(slots, mine, peer, send_sems, recv_sems)):
-            sum_copy(*given, step).start()
-            return carry
-
-        def arrive(step, carry, given=(slots, mine, peer, send_sems, recv_sems)):
-            sum_copy(*given, step).wait_recv()
-            return carry
-
-        lax.fori_loop(1, count, begin, 0)
-        lax.fori_loop(1, count, arrive, 0)
+        for step in far_first(count):
+            sum_copy(slots, mine, peer, send_sems, recv_sems, step).start()
+        for step in range(1, count):
+            sum_copy(slots, mine, peer, send_sems, recv_sems, step).wait_recv()
         row = jnp.sum(slots[...], axis=0)
 
     spreaded = jnp.where(diagonal, jnp.broadcast_to(row, (32, 128)), 0.0)
@@ -551,11 +547,8 @@
             each_copy(turn, index, lambda copy: copy.wait_send())
     for slots, count, mine, peer, send_sems, recv_sems in stages:
 
-        def leave(step, carry, given=(slots, mine, peer, send_sems, recv_sems)):
-            sum_copy(*given, step).wait_send()
-            return carry
-
-        lax.fori_loop(1, count, leave, 0)
+        for step in range(1, count):
+            sum_copy(slots, mine, peer, send_sems, recv_sems, step).wait_send()
 
 
 def solution(mesh):

time: 48.9 us -> 46.3 us (0.947)
  Pallas kernels: 47.5 us -> 45 us
    pallas_call x1, Pallas kernels: 47.5 us -> 45 us  [shards(): pl.pallas_call(functools.partial(kernel, (owners, n_y, n_z)), out_shape=(...]
where the time goes in v2:
time: 46.3 us; the launch traced here: 46.2 us
  Pallas kernels  45 us (97%)
  other arithmetic  1.2 us (3%)
    pallas_call x1, Pallas kernels, shards(): pl.pallas_call(functools.partial(kernel, (owners, n_y, n_z)), out_shape=(...  45 us
    add x1, other arithmetic, shards(): factor[0:COMP, None, :] * first.reshape(shape)  1.2 us

profile of v2, /device:TPU:1, one launch (start us, length us, event | category | flops | bytes accessed | tf_op | source)
XLA Modules:
  0.0 46.2 jit_solution(9831184035430993200)
XLA Ops:
  0.0 45.0 %shard_map.46 = (f32[2560,128]{1,0:T(8,128)S(1)}, f32[2560,128]{1,0:T(8,128)S(1)}, f32[16,128]{1,0:T(8,128)S(1)}) custom-call(f32[2560,128]{1,0:T(8,128)} %bitcast.6, f32[1536,128]{1,0:T(8,128)} %bitcast.7, f32[4,128]{1,0:T(4,128)} %geometry_hbm.1, s32[1,704]{1,0:T(1,128)} %codes_hbm.1), custom_call_target="tpu_custom_call" | custom-call | tf_op jit(solution)/shard_map/pallas_call | solution.py:572
  45.0 1.2 %multiply_add_fusion = f32[5,512,128]{2,1,0:T(8,128)} fusion(f32[5,512,128]{2,1,0:T(8,128)S(1)} %bitcast.5, f32[5,512,128]{2,1,0:T(8,128)S(1)} %bitcast.4, f32[5,128]{1,0:T(8,128)S(1)} %get-tuple-element.12, f32[5,128]{1,0:T(8,128)S(1)} %get-tuple-element.11), kind=kLoop, calls=%fused_computation | loop fusion | flops 983040 | bytes 3937280 | tf_op jit(solution)/shard_map/add | solution.py:618
  (1 shorter events, 0.0 us)

commit v3 on v2

--- a/solution.py
+++ b/solution.py
@@ -96,9 +96,10 @@
     even, odd, sign = table
     sums = [values[a] + values[7 - a] for a in range(4)]
     gaps = [values[a] - values[7 - a] for a in range(4)]
+    steps = [sums[a] - sums[3] for a in range(3)]
     result = [None] * 8
     for i in range(4):
-        first = sum(even[i][a] * sums[a] for a in range(1, 4)) + even[i][0] * sums[0]
+        first = even[i][0] * steps[0] + even[i][1] * steps[1] + even[i][2] * steps[2]
         second = sum(odd[i][a] * gaps[a] for a in range(1, 4)) + odd[i][0] * gaps[0]
         result[i] = first + second
         result[7 - i] = first - second if sign > 0 else second - first
@@ -414,7 +415,7 @@
         for step in far_first(owners):
             act(face_copy(turn, index, step))
 
-    def send(turn, index, field):
+    def select(turn, index, field):
         low, high = GROUPS[index]
 
         def gather(comp, carry):
@@ -436,8 +437,8 @@
         outgoing[turn, index, :, 0 : stop - start] = dot(
             chosen[...], faces[start:stop, :], over_lanes
         ) + dot(chosen[...], faces[HALF_ROWS + start : HALF_ROWS + stop, :], over_lanes)
-        if turn == 0 and index == 0:
-            pl.semaphore_wait(barrier, owners - 1 + n_near - 1 + n_far - 1)
+
+    def start(turn, index):
         each_copy(turn, index, lambda copy: copy.start())
 
     plain_dims = ((1,), (0,))
@@ -449,15 +450,17 @@
                 faces[HALF_ROWS:, :], pairs[:, place], plain_dims
             )
 
+    def wait(turn, index):
+        each_copy(turn, index, lambda copy: copy.wait_recv())
+
     def receive(turn, index, field, quantity):
         low, high = GROUPS[index]
-        start, stop = low * FACE_ROWS, high * FACE_ROWS
-        each_copy(turn, index, lambda copy: copy.wait_recv())
-        big, small = split(jnp.transpose(incoming[turn, index])[0 : stop - start, :])
+        begin, stop = low * FACE_ROWS, high * FACE_ROWS
+        big, small = split(jnp.transpose(incoming[turn, index])[0 : stop - begin, :])
         for part in range(3):
             place = slice(256 * part, 256 * part + 256)
-            gained[start:stop, place] = (
-                gained[start:stop, place]
+            gained[begin:stop, place] = (
+                gained[begin:stop, place]
                 + dot(big, chosen[:, place], plain_dims)
                 + dot(small, chosen[:, place], plain_dims)
             )
@@ -488,15 +491,26 @@
     for index, (low, high) in enumerate(GROUPS):
         loads[3 + index].wait()
         lax.fori_loop(low, high, force, 0, unroll=True)
-        send(0, index, first)
+        select(0, index, first)
+        if index == 0:
+            pl.semaphore_wait(barrier, owners - 1 + n_near - 1 + n_far - 1)
+        start(0, index)
     build_pairs()
     local()
+    last = len(GROUPS) - 1
     for index, (low, high) in enumerate(GROUPS):
+        wait(0, index)
+        if index > 0:
+            select(1, index - 1, image)
         receive(0, index, first, 0)
+        if index > 0:
+            start(1, index - 1)
         lax.fori_loop(low, high, spread, 0, unroll=True)
-        send(1, index, image)
+    select(1, last, image)
+    start(1, last)
     local()
     for index, (low, high) in enumerate(GROUPS):
+        wait(1, index)
         receive(1, index, image, 2)
         lax.fori_loop(low, high, energy, 0, unroll=True)
 
@@ -525,7 +539,13 @@
 
         for step in far_first(count):
             sum_copy(slots, mine, peer, send_sems, recv_sems, step).start()
-        for step in range(1, count):
+        if slots is near_slots:
+            for turn in range(2):
+                for index in range(len(GROUPS)):
+                    each_copy(turn, index, lambda copy: copy.wait_send())
+        for step in far_first(count):
+            sum_copy(slots, mine, peer, send_sems, recv_sems, step).wait_send()
+        for step in reversed(far_first(count)):
             sum_copy(slots, mine, peer, send_sems, recv_sems, step).wait_recv()
         row = jnp.sum(slots[...], axis=0)
 
@@ -541,14 +561,6 @@
     alpha_next = norm_next / curve
     factor_ref[0:8, :] = alpha + alpha_next * up
     factor_ref[8:16, :] = -alpha * alpha_next
-
-    for turn in range(2):
-        for index in range(len(GROUPS)):
-            each_copy(turn, index, lambda copy: copy.wait_send())
-    for slots, count, mine, peer, send_sems, recv_sems in stages:
-
-        for step in range(1, count):
-            sum_copy(slots, mine, peer, send_sems, recv_sems, step).wait_send()
 
 
 def solution(mesh):

time: 46.3 us -> 45.6 us (0.985)
  Pallas kernels: 45 us -> 44.3 us
    pallas_call x1, Pallas kernels: 45 us -> 44.3 us  [shards(): pl.pallas_call(functools.partial(kernel, (owners, n_y, n_z)), out_shape=(...]
where the time goes in v3:
time: 45.6 us; the launch traced here: 45.5 us
  Pallas kernels  44.3 us (97%)
  other arithmetic  1.2 us (3%)
    pallas_call x1, Pallas kernels, shards(): pl.pallas_call(functools.partial(kernel, (owners, n_y, n_z)), out_shape=(...  44.3 us
    add x1, other arithmetic, shards(): factor[0:COMP, None, :] * first.reshape(shape)  1.2 us

profile of v3, /device:TPU:1, one launch (start us, length us, event | category | flops | bytes accessed | tf_op | source)
XLA Modules:
  0.0 45.5 jit_solution(7903954375623404101)
XLA Ops:
  0.0 44.3 %shard_map.46 = (f32[2560,128]{1,0:T(8,128)S(1)}, f32[2560,128]{1,0:T(8,128)S(1)}, f32[16,128]{1,0:T(8,128)S(1)}) custom-call(f32[2560,128]{1,0:T(8,128)} %bitcast.6, f32[1536,128]{1,0:T(8,128)} %bitcast.7, f32[4,128]{1,0:T(4,128)} %geometry_hbm.1, s32[1,704]{1,0:T(1,128)} %codes_hbm.1), custom_call_target="tpu_custom_call" | custom-call | tf_op jit(solution)/shard_map/pallas_call | solution.py:584
  44.3 1.2 %multiply_add_fusion = f32[5,512,128]{2,1,0:T(8,128)} fusion(f32[5,512,128]{2,1,0:T(8,128)S(1)} %bitcast.5, f32[5,512,128]{2,1,0:T(8,128)S(1)} %bitcast.4, f32[5,128]{1,0:T(8,128)S(1)} %get-tuple-element.12, f32[5,128]{1,0:T(8,128)S(1)} %get-tuple-element.11), kind=kLoop, calls=%fused_computation | loop fusion | flops 983040 | bytes 3937280 | tf_op jit(solution)/shard_map/add | solution.py:630
  (1 shorter events, 0.0 us)

commit v4 on v3

--- a/solution.py
+++ b/solution.py
@@ -261,11 +261,8 @@
             chosen[16 * block : 16 * block + 16, 128 * face : 128 * face + 128] = jnp.where(
                 code == lane16 + float(128 * face), 1.0, 0.0
             ).astype(jnp.bfloat16)
-    for turn in range(2):
-        own = pl.ds(pl.multiple_of(me * FMAX, FMAX), FMAX)
-        for index in range(len(GROUPS)):
-            outgoing[turn, index] = jnp.zeros((128, 128), jnp.float32)
-            incoming[turn, index, own, :] = jnp.zeros((FMAX, 128), jnp.float32)
+    for index in range(len(GROUPS)):
+        outgoing[0, index] = jnp.zeros((128, 128), jnp.float32)
 
     loads[1].wait()
     volume = jnp.broadcast_to(geometry[0:1, :], (8, 128))
@@ -495,6 +492,11 @@
         if index == 0:
             pl.semaphore_wait(barrier, owners - 1 + n_near - 1 + n_far - 1)
         start(0, index)
+    own = pl.ds(pl.multiple_of(me * FMAX, FMAX), FMAX)
+    for index in range(len(GROUPS)):
+        outgoing[1, index] = jnp.zeros((128, 128), jnp.float32)
+        for turn in range(2):
+            incoming[turn, index, own, :] = jnp.zeros((FMAX, 128), jnp.float32)
     build_pairs()
     local()
     last = len(GROUPS) - 1

time: 45.6 us -> 45.6 us (level)
  no operation moved by 1% of the time
where the time goes in v4:
time: 45.6 us; the launch traced here: 45.5 us
  Pallas kernels  44.3 us (97%)
  other arithmetic  1.2 us (3%)
    pallas_call x1, Pallas kernels, shards(): pl.pallas_call(functools.partial(kernel, (owners, n_y, n_z)), out_shape=(...  44.3 us
    add x1, other arithmetic, shards(): factor[0:COMP, None, :] * first.reshape(shape)  1.2 us

profile of v4, /device:TPU:1, one launch (start us, length us, event | category | flops | bytes accessed | tf_op | source)
XLA Modules:
  0.0 45.5 jit_solution(5708089569088828836)
XLA Ops:
  0.0 44.3 %shard_map.46 = (f32[2560,128]{1,0:T(8,128)S(1)}, f32[2560,128]{1,0:T(8,128)S(1)}, f32[16,128]{1,0:T(8,128)S(1)}) custom-call(f32[2560,128]{1,0:T(8,128)} %bitcast.6, f32[1536,128]{1,0:T(8,128)} %bitcast.7, f32[4,128]{1,0:T(4,128)} %geometry_hbm.1, s32[1,704]{1,0:T(1,128)} %codes_hbm.1), custom_call_target="tpu_custom_call" | custom-call | tf_op jit(solution)/shard_map/pallas_call | solution.py:586
  44.3 1.2 %multiply_add_fusion = f32[5,512,128]{2,1,0:T(8,128)} fusion(f32[5,512,128]{2,1,0:T(8,128)S(1)} %bitcast.5, f32[5,512,128]{2,1,0:T(8,128)S(1)} %bitcast.4, f32[5,128]{1,0:T(8,128)S(1)} %get-tuple-element.12, f32[5,128]{1,0:T(8,128)S(1)} %get-tuple-element.11), kind=kLoop, calls=%fused_computation | loop fusion | flops 983040 | bytes 3937280 | tf_op jit(solution)/shard_map/add | solution.py:632
  (1 shorter events, 0.0 us)
